TPU v7x, 32 devices: a whole 2x2x4 slice. The times are simulated.
32 devices in a mesh: leaf: 8 (over z, x), panel: 4 (over y, core).
Axes of the slice: x: 2, y: 2, z: 4, core: 2. Of those that a mesh axis runs over, the one named last changes fastest.
Arguments:
- child_front: float32 [8, 2048, 2048], P('leaf', 'panel'), as said below
- child_panel: bfloat16 [8, 2048, 4096], P('leaf'), may hold values from -0.03125 to 0.03125
- parent_front: float32 [4096, 4096], P('leaf', 'panel'), as said below
- tile_map: int32 [8, 8], P('leaf'), may hold values from 0 to 15, as said below
- tile_count: int32 [8], P('leaf'), may hold values from 2 to 8, as said below
Outputs:
- eliminated: float32 [4096, 4096], P('leaf', 'panel')
Inputs may be any that keep to these rules, and one draw needn't show every extreme that they name: `tile_count`: some child has 8 live tiles and some child has 2. `tile_map`: for child c the first tile_count[c] entries are distinct and rising; the other entries are 0. Each child's block is symmetric, and child_front[c] - child_panel[c] child_panel[c]^T is positive definite. `parent_front`: symmetric positive definite.
All inputs are finite; a program needn't handle non-finite values.
Results may differ from a plain program's by a relative error of at most 0.0003.
Values sent between devices are 32-bit elements; how exact they have to be, the bound alone decides.
A program may use at most 128 MiB of HBM per device.

v0:
```python
import jax
import jax.numpy as jnp
from jax import lax
from jax.sharding import PartitionSpec as P

TILE = 256
NF = 4096
CB = 2048
STEPS = 4


def spread(array, axis, root):
    mine = lax.axis_index(axis) == root
    return lax.psum(jnp.where(mine, array, jnp.zeros_like(array)), axis)


def finish_rows(block, row_index, factor, pivot_start):
    solved = lax.linalg.triangular_solve(
        factor, block, left_side=False, lower=True, transpose_a=True
    )
    offset = jnp.clip(row_index - pivot_start, 0, TILE - 1)
    own_rows = jnp.take(factor, offset, axis=0)
    inside = (row_index >= pivot_start) & (row_index < pivot_start + TILE)
    kept = jnp.where(inside[:, None], own_rows, solved)
    return jnp.where(row_index[:, None] < pivot_start, 0.0, kept)


def shards(child_front, child_panel, parent_front, tile_map, tile_count):
    highest = lax.Precision.HIGHEST
    panel_count = lax.axis_size("panel")
    leaf_id = lax.axis_index("leaf")
    panel_id = lax.axis_index("panel")
    tiles_child = CB // TILE
    tiles_front = NF // TILE
    pivot_span = STEPS * TILE
    child_rows = child_front.shape[1]
    height = parent_front.shape[0]
    col_width = parent_front.shape[1]
    panel_all = child_panel[0]
    own_panel = lax.dynamic_slice_in_dim(panel_all, panel_id * child_rows, child_rows, 0)
    update = child_front[0] - lax.dot_general(
        own_panel, panel_all, (((1,), (1,)), ((), ())), preferred_element_type=jnp.float32
    )
    mapped = tile_map[0]
    live_tiles = jnp.arange(tiles_child, dtype=jnp.int32) < tile_count[0]
    everywhere = jnp.arange(tiles_front, dtype=jnp.int32)
    chosen = ((mapped[None, :] == everywhere[:, None]) & live_tiles[None, :]).astype(jnp.float32)
    placed = jnp.einsum(
        "rtb,ft->rfb", update.reshape(child_rows, tiles_child, TILE), chosen, precision=highest
    )
    placed = placed.reshape(child_rows, panel_count, col_width)
    moved_cols = lax.all_to_all(placed, "panel", split_axis=1, concat_axis=0, tiled=True)
    column_tiles = moved_cols.reshape(tiles_child, TILE, col_width)
    targets = jnp.arange(lax.axis_size("leaf") * height // TILE, dtype=jnp.int32)
    picked = ((mapped[None, :] == targets[:, None]) & live_tiles[None, :]).astype(jnp.float32)
    front_block = parent_front + lax.psum_scatter(
        jnp.einsum("ft,tbc->fbc", picked, column_tiles, precision=highest).reshape(
            lax.axis_size("leaf") * height, col_width
        ),
        "leaf",
        scatter_dimension=0,
        tiled=True,
    )
    global_rows = leaf_id * height + jnp.arange(height, dtype=jnp.int32)
    global_cols = panel_id * col_width + jnp.arange(col_width, dtype=jnp.int32)
    col_tiles = col_width // TILE
    for pivot_step in range(STEPS):
        source_panel = pivot_step // col_tiles
        local_start = pivot_step % col_tiles * TILE
        pivot_start = pivot_step * TILE
        source = front_block[:, local_start : local_start + TILE]
        column = spread(source, "panel", source_panel)
        full_column = lax.all_gather(column, "leaf", axis=0, tiled=True)
        factor = jnp.linalg.cholesky(full_column[pivot_start : pivot_start + TILE])
        own_factor = finish_rows(column, global_rows, factor, pivot_start)
        col_factor = finish_rows(
            lax.dynamic_slice_in_dim(full_column, panel_id * col_width, col_width, 0),
            global_cols,
            factor,
            pivot_start,
        )
        front_block = front_block - lax.dot_general(
            own_factor,
            col_factor,
            (((1,), (1,)), ((), ())),
            precision=highest,
            preferred_element_type=jnp.float32,
        )
        replaced = jnp.where(
            panel_id == source_panel, own_factor, front_block[:, local_start : local_start + TILE]
        )
        front_block = front_block.at[:, local_start : local_start + TILE].set(replaced)
    upper_zone = (global_rows[:, None] < pivot_span) & (global_cols[None, :] >= pivot_span)
    return jnp.where(upper_zone, 0.0, front_block)


def solution(mesh):
    placed = (
        P("leaf", "panel", None),
        P("leaf", None, None),
        P("leaf", "panel"),
        P("leaf", None),
        P("leaf"),
    )
    return jax.shard_map(
        shards, mesh=mesh, in_specs=placed, out_specs=P("leaf", "panel"), check_vma=False
    )
```

profile of v0, /device:TPU:0, one launch (start us, length us, event | category | flops | bytes accessed | tf_op | source)
XLA Modules:
  0.0 1247.7 jit_solution(15708329667219929807)
XLA Ops:
  6.5 17.1 %bitcast_subtract_fusion = f32[512,2048]{1,0:T(8,128)S(1)} fusion(f32[1,512,2048]{2,1,0:T(8,128)} %param.22, bf16[1,2048,4096]{2,1,0:T(8,128)(2,1)} %param.23, s32[]{:T(128)S(6)} %select_n.118), kind=kOutput, calls=%fused_computation.19 | convolution fusion | flops 8590983168 | bytes 29360132 | tf_op jit(solution)/shard_map/dot_general | solution.py:41
  51.4 97.1 %all_to_all.15 = f32[512,4,1024]{2,0,1:T(8,128)} all-to-all(f32[512,4,1024]{2,0,1:T(8,128)S(1)} %copy.25), channel_id=1, replica_groups=mesh['leaf'=8,'panel'=4] {'panel'}, dimensions={1} | all-to-all | bytes 16777216 | tf_op jit(solution)/shard_map/all_to_all | solution.py:52
  167.0 19.1 %copy.54 = f32[128,8,16,256]{3,1,2,0:T(8,128)} copy(f32[128,8,16,256]{3,2,1,0:T(8,128)S(1)} %bitcast.202) | data formatting | bytes 33554432
  188.0 282.7 %reduce-scatter.2.cloned.1.call-done = f32[512,1024]{0,1:T(8,128)} async-done(((f32[4096,1024]{0,1:T(8,128)}), f32[512,1024]{0,1:T(8,128)}) %reduce-scatter.2.cloned.1.call-update) | async-done | bytes 2097168 | tf_op jit(solution)/shard_map/reduce_scatter | solution.py:56
  475.0 32.3 %all-reduce.6.cloned.1.call-done = f32[512,256]{0,1:T(8,128)} async-done(((f32[512,256]{0,1:T(8,128)}), f32[512,256]{0,1:T(8,128)}) %all-reduce.6.cloned.1.call-update) | async-done | bytes 524304 | tf_op jit(solution)/shard_map/psum | solution.py:14
  508.4 74.8 %all-gather.5.cloned.1.call-done = f32[4096,256]{0,1:T(8,128)} async-done(((f32[512,256]{0,1:T(8,128)}), f32[4096,256]{0,1:T(8,128)}) %all-gather.5.cloned.1.call-update) | async-done | bytes 4194320 | tf_op jit(solution)/shard_map/all_gather | solution.py:73
  585.2 11.7 cholesky.214
  607.3 11.7 cholesky.231
  625.3 20.1 %custom-call.24 = f32[2,128,128]{1,2,0:T(8,128)S(1)} custom-call(f32[2,128,128]{2,1,0:T(8,128)S(1)} %get-tuple-element.110), custom_call_target="InvertDiagBlocksLowerTriangular" | custom-call | tf_op jit(solution)/shard_map/triangular_solve/custom-call.0 | solution.py:18
  664.8 31.5 %all-reduce.8.cloned.1.call-done = f32[512,256]{0,1:T(8,128)} async-done(((f32[512,256]{0,1:T(8,128)}), f32[512,256]{0,1:T(8,128)}) %all-reduce.8.cloned.1.call-update) | async-done | bytes 524304 | tf_op jit(solution)/shard_map/psum | solution.py:14
  699.0 73.0 %all-gather.7.cloned.1.call-done = f32[4096,256]{0,1:T(8,128)} async-done(((f32[512,256]{0,1:T(8,128)}), f32[4096,256]{0,1:T(8,128)}) %all-gather.7.cloned.1.call-update) | async-done | bytes 4194320 | tf_op jit(solution)/shard_map/all_gather | solution.py:73
  774.1 11.7 cholesky.248
  796.1 11.7 cholesky.265
  815.4 19.9 %custom-call.27 = f32[2,128,128]{1,2,0:T(8,128)S(1)} custom-call(f32[2,128,128]{2,1,0:T(8,128)S(1)} %get-tuple-element.112), custom_call_target="InvertDiagBlocksLowerTriangular" | custom-call | tf_op jit(solution)/shard_map/triangular_solve/custom-call.0 | solution.py:18
  857.2 31.6 %all-reduce.10.cloned.1.call-done = f32[512,256]{0,1:T(8,128)} async-done(((f32[512,256]{0,1:T(8,128)}), f32[512,256]{0,1:T(8,128)}) %all-reduce.10.cloned.1.call-update) | async-done | bytes 524304 | tf_op jit(solution)/shard_map/psum | solution.py:14
  890.0 74.6 %all-gather.9.cloned.1.call-done = f32[4096,256]{0,1:T(8,128)} async-done(((f32[512,256]{0,1:T(8,128)}), f32[4096,256]{0,1:T(8,128)}) %all-gather.9.cloned.1.call-update) | async-done | bytes 4194320 | tf_op jit(solution)/shard_map/all_gather | solution.py:73
  966.7 11.7 cholesky.282
  988.8 11.7 cholesky.299
  1007.4 19.8 %custom-call.30 = f32[2,128,128]{1,2,0:T(8,128)S(1)} custom-call(f32[2,128,128]{2,1,0:T(8,128)S(1)} %get-tuple-element.114), custom_call_target="InvertDiagBlocksLowerTriangular" | custom-call | tf_op jit(solution)/shard_map/triangular_solve/custom-call.0 | solution.py:18
  1049.4 31.3 %all-reduce.12.cloned.1.call-done = f32[512,256]{0,1:T(8,128)} async-done(((f32[512,256]{0,1:T(8,128)}), f32[512,256]{0,1:T(8,128)}) %all-reduce.12.cloned.1.call-update) | async-done | bytes 524304 | tf_op jit(solution)/shard_map/psum | solution.py:14
  1083.1 73.5 %all-gather.11.cloned.1.call-done = f32[4096,256]{0,1:T(8,128)} async-done(((f32[512,256]{0,1:T(8,128)}), f32[4096,256]{0,1:T(8,128)}) %all-gather.11.cloned.1.call-update) | async-done | bytes 4194320 | tf_op jit(solution)/shard_map/all_gather | solution.py:73
  1158.7 11.7 cholesky.316
  1180.8 11.7 cholesky.333
  1199.7 19.7 %custom-call.33 = f32[2,128,128]{1,2,0:T(8,128)S(1)} custom-call(f32[2,128,128]{2,1,0:T(8,128)S(1)} %get-tuple-element.116), custom_call_target="InvertDiagBlocksLowerTriangular" | custom-call | tf_op jit(solution)/shard_map/triangular_solve/custom-call.0 | solution.py:18
  (262 shorter events, 231.8 us)
Async XLA Ops:
  6.5 464.2 %reduce-scatter.2.cloned.1.call-start = ((), (), s32[]{:S(2)}) async-start(), calls=%async_computation.2 | async-start | bytes 18874368 | tf_op jit(solution)/shard_map/reduce_scatter | solution.py:56
  186.0 321.3 %all-reduce.6.cloned.1.call-start = ((), (), s32[]{:S(2)}) async-start(), calls=%async_computation.3 | async-start | bytes 1048576 | tf_op jit(solution)/shard_map/psum | solution.py:14
  475.0 108.2 %all-gather.5.cloned.1.call-start = ((), (), s32[]{:S(2)}) async-start(), calls=%async_computation.4 | async-start | bytes 4718592 | tf_op jit(solution)/shard_map/all_gather | solution.py:73
  507.3 138.1 %copy-start.17 = (f32[512,256]{0,1:T(8,128)S(1)}, f32[512,256]{0,1:T(8,128)}, u32[]{:S(2)}) copy-start(f32[512,256]{0,1:T(8,128)} %all-reduce.6.cloned.1.call-done) | copy-start | bytes 1572868
  507.3 189.0 %all-reduce.8.cloned.1.call-start = ((), (), s32[]{:S(2)}) async-start(), calls=%async_computation.5 | async-start | bytes 1048576 | tf_op jit(solution)/shard_map/psum | solution.py:14
  645.8 5.0 copy-start.7
  664.7 107.3 %all-gather.7.cloned.1.call-start = ((), (), s32[]{:S(2)}) async-start(), calls=%async_computation.6 | async-start | bytes 4718592 | tf_op jit(solution)/shard_map/all_gather | solution.py:73
  696.3 139.0 %copy-start.20 = (f32[512,256]{0,1:T(8,128)S(1)}, f32[512,256]{0,1:T(8,128)}, u32[]{:S(2)}) copy-start(f32[512,256]{0,1:T(8,128)} %all-reduce.8.cloned.1.call-done) | copy-start | bytes 1572868
  696.3 192.5 %all-reduce.10.cloned.1.call-start = ((), (), s32[]{:S(2)}) async-start(), calls=%async_computation.7 | async-start | bytes 1048576 | tf_op jit(solution)/shard_map/psum | solution.py:14
  815.4 21.9 %copy-start.22 = (f32[256,256]{1,0:T(8,128)}, f32[256,256]{1,0:T(8,128)S(1)}, u32[]{:S(2)}) copy-start(f32[256,256]{1,0:T(8,128)S(1)} %get-tuple-element.424) | copy-start | bytes 786436
  843.8 6.7 copy-start.27
  849.1 4.9 copy-start.29
  854.1 149.2 %copy-start.32 = (s32[2,2]{1,0:T(2,128)S(1)}, s32[2,2]{1,0:T(2,128)}, u32[]{:S(2)}) copy-start(s32[2,2]{1,0:T(2,128)} %copy-done.31) | copy-start | bytes 52
  857.2 107.4 %all-gather.9.cloned.1.call-start = ((), (), s32[]{:S(2)}) async-start(), calls=%async_computation.8 | async-start | bytes 4718592 | tf_op jit(solution)/shard_map/all_gather | solution.py:73
  888.8 138.4 %copy-start.19 = (f32[512,256]{0,1:T(8,128)S(1)}, f32[512,256]{0,1:T(8,128)}, u32[]{:S(2)}) copy-start(f32[512,256]{0,1:T(8,128)} %all-reduce.10.cloned.1.call-done) | copy-start | bytes 1572868
  888.8 191.9 %all-reduce.12.cloned.1.call-start = ((), (), s32[]{:S(2)}) async-start(), calls=%async_computation.9 | async-start | bytes 1048576 | tf_op jit(solution)/shard_map/psum | solution.py:14
  1035.7 6.8 copy-start.1
  1049.2 107.4 %all-gather.11.cloned.1.call-start = ((), (), s32[]{:S(2)}) async-start(), calls=%async_computation.10 | async-start | bytes 4718592 | tf_op jit(solution)/shard_map/all_gather | solution.py:73
  1080.8 138.7 %copy-start.18 = (f32[512,256]{0,1:T(8,128)S(1)}, f32[512,256]{0,1:T(8,128)}, u32[]{:S(2)}) copy-start(f32[512,256]{0,1:T(8,128)} %all-reduce.12.cloned.1.call-done) | copy-start | bytes 1572868
  1199.7 21.7 %copy-start.21 = (f32[256,256]{1,0:T(8,128)}, f32[256,256]{1,0:T(8,128)S(1)}, u32[]{:S(2)}) copy-start(f32[256,256]{1,0:T(8,128)S(1)} %get-tuple-element.422) | copy-start | bytes 786436
  1227.9 6.8 copy-start.3
  1233.4 5.0 copy-start.24
  1233.4 5.0 copy-start.25
  1233.4 5.0 copy-start.26
  (18 other events, 55.3 us)
Sparse Core Ops, SparseCore 0:
  186.2 284.4 reduce-scatter.1
  475.1 32.1 all-reduce.5
  509.7 73.3 all-gather.4
  664.8 31.4 all-reduce.7
  698.6 73.3 all-gather.6
  857.3 31.4 all-reduce.9
  891.2 73.3 all-gather.8
  1049.3 31.4 all-reduce.11
  1083.2 73.3 all-gather.10
where the time goes:
time: 1260 us; the launch traced here: 1250 us
  waiting for transfers between devices  705 us (56%)
  other arithmetic  237 us (19%)
  local copies, waits for them, and re-layouts  110 us (9%)
  blocking collectives  97.1 us (8%)
  matrix products  76.3 us (6%)
  between operations  20.6 us (2%)
    all_gather x4, waiting for transfers between devices, shards(): full_column = lax.all_gather(column, 'leaf', axis=0, tiled=True)  296 us
    reduce_scatter x1, waiting for transfers between devices, shards(): lax.psum_scatter(jnp.einsum('ft,tbc->fbc', picked, column_tiles, precisio...  283 us
    another operation x27, other arithmetic, shards(): factor = jnp.linalg.cholesky(full_column[pivot_start:pivot_start + TILE])  138 us
    psum x4, waiting for transfers between devices, spread(): return lax.psum(jnp.where(mine, array, jnp.zeros_like(array)), axis)  127 us
    all_to_all x1, blocking collectives, shards(): lax.all_to_all(placed, 'panel', split_axis=1, concat_axis=0, tiled=True)  97.1 us
    another operation x9, other arithmetic, finish_rows(): lax.linalg.triangular_solve(factor, block, left_side=False, lower=True, t...  79.6 us
    gather x16, local copies, waits for them, and re-layouts, finish_rows(): own_rows = jnp.take(factor, offset, axis=0)  31.5 us
    unnamed x69, local copies, waits for them, and re-layouts  27.6 us
  transfers between devices with their start and end apart: 9, of which 9 were waited for; matrix products, arithmetic and copies ran while one was open for 1% of the time, Pallas kernels for 0%

commit v1 on v0

v1 whole, which is shorter than its diff:
```python
import functools

import jax
import jax.numpy as jnp
from jax import lax
from jax.experimental import pallas as pl
from jax.experimental.pallas import tpu as pltpu
from jax.sharding import PartitionSpec as P

TILE = 256
STEPS = 4
SPAN = STEPS * TILE
HIGH = lax.Precision.HIGH


def mm(a, b, dims):
    return lax.dot_general(a, b, (dims, ((), ())), precision=HIGH, preferred_element_type=jnp.float32)


def copy_tile(index, live, src, dst):
    f = pl.program_id(0)

    @pl.when(live[f] > 0)
    def _():
        dst[...] = src[...].reshape(dst.shape)

    @pl.when(live[f] == 0)
    def _():
        dst[...] = jnp.zeros_like(dst)


def place_columns(update, index, live, panels):
    rows = update.shape[0]
    count = index.shape[0]
    per = count // panels
    return pl.pallas_call(
        copy_tile,
        out_shape=jax.ShapeDtypeStruct((panels, rows, per * TILE), jnp.float32),
        grid_spec=pltpu.PrefetchScalarGridSpec(
            num_scalar_prefetch=2,
            grid=(count,),
            in_specs=[pl.BlockSpec((rows, TILE), lambda f, index, live: (0, index[f]))],
            out_specs=pl.BlockSpec((1, rows, TILE), lambda f, index, live: (f // per, 0, f % per)),
        ),
        cost_estimate=pl.CostEstimate(flops=0, bytes_accessed=12 * rows * 2048, transcendentals=0),
    )(index, live, update)


def place_rows(tiles, index, live):
    count = index.shape[0]
    width = tiles.shape[2]
    return pl.pallas_call(
        copy_tile,
        out_shape=jax.ShapeDtypeStruct((count, TILE, width), jnp.float32),
        grid_spec=pltpu.PrefetchScalarGridSpec(
            num_scalar_prefetch=2,
            grid=(count,),
            in_specs=[pl.BlockSpec((1, TILE, width), lambda f, index, live: (index[f], 0, 0))],
            out_specs=pl.BlockSpec((1, TILE, width), lambda f, index, live: (f, 0, 0)),
        ),
        cost_estimate=pl.CostEstimate(flops=0, bytes_accessed=8 * count * TILE * width, transcendentals=0),
    )(index, live, tiles).reshape(count * TILE, width)


def factorize(top):
    eye = jnp.eye(TILE, dtype=jnp.float32)
    work = top
    columns, inverses = [], []
    for _ in range(STEPS):
        diag = jnp.linalg.cholesky(work[:TILE, :TILE])
        inv = lax.linalg.triangular_solve(diag, eye, left_side=True, lower=True)
        lower = mm(work[TILE:, :TILE], inv, ((1,), (1,)))
        work = work[TILE:, TILE:] - mm(lower, lower, ((1,), (1,)))
        columns.append((diag, lower))
        inverses.append(inv)
    return columns, inverses


def shards(child_front, child_panel, parent_front, tile_map, tile_count):
    leaves, panels = lax.axis_size("leaf"), lax.axis_size("panel")
    leaf_id, panel_id = lax.axis_index("leaf"), lax.axis_index("panel")
    child_rows, order = child_front.shape[1:]
    height, width = parent_front.shape
    child_tiles, front_tiles = order // TILE, leaves * height // TILE
    own_tiles = child_rows // TILE
    row_start, col_start = leaf_id * height, panel_id * width
    is_top, is_left = row_start < SPAN, col_start < SPAN

    panel_all = child_panel[0]
    own_panel = lax.dynamic_slice_in_dim(panel_all, panel_id * child_rows, child_rows, 0)
    update = child_front[0] - lax.dot_general(
        own_panel, panel_all, (((1,), (1,)), ((), ())), preferred_element_type=jnp.float32
    )
    targets = jnp.arange(front_tiles, dtype=jnp.int32)
    positions = jnp.arange(child_tiles, dtype=jnp.int32)
    hit = (tile_map[0][None, :] == targets[:, None]) & (positions < tile_count[0])[None, :]
    live = jnp.any(hit, axis=1).astype(jnp.int32)
    index = jnp.sum(jnp.where(hit, positions[None, :], 0), axis=1).astype(jnp.int32)

    placed = place_columns(update, index, live, panels)
    pivot_panels = SPAN // width
    left = jnp.concatenate([placed[i] for i in range(pivot_panels)], axis=1)
    own = index[:STEPS] - panel_id * own_tiles
    held = (live[:STEPS] > 0) & (own >= 0) & (own < own_tiles)
    top_part = place_rows(
        left.reshape(own_tiles, TILE, SPAN),
        jnp.where(held, own, 0).astype(jnp.int32),
        held.astype(jnp.int32),
    )
    own_top = jnp.where(is_top & is_left, parent_front, 0.0)
    row_clip = jnp.where(is_top, row_start, 0)
    col_clip = jnp.where(is_left, col_start, 0)
    old = lax.dynamic_slice(top_part, (row_clip, col_clip), (height, width))
    top_part = lax.dynamic_update_slice(top_part, old + own_top, (row_clip, col_clip))
    top = lax.psum(top_part, ("leaf", "panel"))

    moved = lax.all_to_all(placed, "panel", split_axis=0, concat_axis=0, tiled=True)
    moved = moved.reshape(child_tiles, TILE, width)
    pivot_part = place_rows(moved, index[:STEPS], live[:STEPS])
    old = lax.dynamic_slice(pivot_part, (row_clip, 0), (height, width))
    pivot_part = lax.dynamic_update_slice(
        pivot_part, old + jnp.where(is_top, parent_front, 0.0), (row_clip, 0)
    )
    pivot_rows = lax.psum(pivot_part, "leaf")
    expanded = place_rows(moved, index, live)
    front_block = parent_front + lax.psum_scatter(expanded, "leaf", scatter_dimension=0, tiled=True)

    mine = lax.dynamic_slice(pivot_rows, (0, lax.rem(row_start, width)), (SPAN, height))
    source = [l * height // width for l in range(leaves)]
    own_cols = mine
    for shift in range(1, panels):
        pairs = [
            (l * panels + source[l], l * panels + (source[l] + shift) % panels) for l in range(leaves)
        ]
        got = lax.ppermute(mine, ("leaf", "panel"), pairs)
        holder = row_start // width
        own_cols = jnp.where(lax.rem(holder + shift, panels) == panel_id, got, own_cols)

    columns, inverses = factorize(top)
    rhs = jnp.concatenate([pivot_rows, own_cols], axis=1)
    solved = []
    for k in range(STEPS):
        solved.append(mm(inverses[k], rhs[:TILE], ((1,), (0,))))
        if k < STEPS - 1:
            rhs = rhs[TILE:] - mm(columns[k][1], solved[k], ((1,), (0,)))
    solved = jnp.concatenate(solved, axis=0)
    below_cols, below_rows = solved[:, :width], solved[:, width:]
    rest = front_block - mm(below_rows, below_cols, ((0,), (0,)))

    factor = jnp.concatenate(
        [
            jnp.concatenate([jnp.zeros((k * TILE, TILE), jnp.float32), diag, lower], axis=0)
            for k, (diag, lower) in enumerate(columns)
        ],
        axis=1,
    )
    factor_part = lax.dynamic_slice(factor, (row_clip, col_clip), (height, width))
    below_part = lax.dynamic_slice(below_rows, (col_clip, 0), (width, height)).T
    left_part = jnp.where(is_top, factor_part, below_part)
    right_part = jnp.where(is_top, 0.0, rest)
    return jnp.where(is_left, left_part, right_part)


def solution(mesh):
    placed = (
        P("leaf", "panel", None),
        P("leaf", None, None),
        P("leaf", "panel"),
        P("leaf", None),
        P("leaf"),
    )
    return jax.shard_map(
        shards, mesh=mesh, in_specs=placed, out_specs=P("leaf", "panel"), check_vma=False
    )
```

time: 1260 us -> 769 us (0.61)
  waiting for transfers between devices: 705 us -> 310 us
  blocking collectives: 97.1 us -> 0 us
  Pallas kernels: 0 us -> 37.5 us
  local copies, waits for them, and re-layouts: 110 us -> 78 us
  matrix products: 76.3 us -> 56.7 us
  starting transfers between devices: 0.54 us -> 15.5 us
    all_gather x4 -> x0, waiting for transfers between devices: 296 us -> none  [shards(): full_column = lax.all_gather(column, 'leaf', axis=0, tiled=True)]
    reduce_scatter x1, waiting for transfers between devices: 283 us -> 121 us  [shards(): lax.psum_scatter(expanded, 'leaf', scatter_dimension=0, tiled=True)]
    all_to_all x1 -> x0, blocking collectives: 97.1 us -> none  [shards(): lax.all_to_all(placed, 'panel', split_axis=1, concat_axis=0, tiled=True)]
    all_to_all x0 -> x1, waiting for transfers between devices: none -> 76.1 us  [shards(): lax.all_to_all(placed, 'panel', split_axis=0, concat_axis=0, tiled=True)]
    pallas_call x0 -> x4, Pallas kernels: none -> 37.5 us  [the longest x3 25.8 us: place_rows(): pl.pallas_call(copy_tile, out_shape=jax.ShapeDtypeStruct((count, TILE, wi...]
    gather x16 -> x0, local copies, waits for them, and re-layouts: 31.5 us -> none  [finish_rows(): own_rows = jnp.take(factor, offset, axis=0)]
    psum x4 -> x2, waiting for transfers between devices: 127 us -> 106 us  [the longest x1 106 us: shards(): top = lax.psum(top_part, ('leaf', 'panel'))]
    unnamed x69 -> x42, local copies, waits for them, and re-layouts: 27.6 us -> 7.2 us
  transfers between devices with their start and end apart: 9 -> 7, of which waited for: 9 -> 4; matrix products, arithmetic and copies ran while one was open for 1% -> 43% of each run, Pallas kernels for 0% -> 3%
where the time goes in v1:
time: 769 us; the launch traced here: 759 us
  waiting for transfers between devices  310 us (40%)
  other arithmetic  241 us (31%)
  local copies, waits for them, and re-layouts  78 us (10%)
  matrix products  56.7 us (7%)
  Pallas kernels  37.5 us (5%)
  between operations  20 us (3%)
  starting transfers between devices  15.5 us (2%)
    another operation x27, other arithmetic, factorize(): diag = jnp.linalg.cholesky(work[:TILE, :TILE])  145 us
    reduce_scatter x1, waiting for transfers between devices, shards(): lax.psum_scatter(expanded, 'leaf', scatter_dimension=0, tiled=True)  121 us
    psum x1, waiting for transfers between devices, shards(): top = lax.psum(top_part, ('leaf', 'panel'))  106 us
    another operation x9, other arithmetic, factorize(): inv = lax.linalg.triangular_solve(diag, eye, left_side=True, lower=True)  82.2 us
    all_to_all x1, waiting for transfers between devices, shards(): lax.all_to_all(placed, 'panel', split_axis=0, concat_axis=0, tiled=True)  76.1 us
    dot_general x14, matrix products, mm(): lax.dot_general(a, b, (dims, ((), ())), precision=HIGH, preferred_element...  27.9 us
    pallas_call x3, Pallas kernels, place_rows(): pl.pallas_call(copy_tile, out_shape=jax.ShapeDtypeStruct((count, TILE, wi...  25.8 us
    reshape x2, local copies, waits for them, and re-layouts, place_rows(): return pl.pallas_call(copy_tile, out_shape=jax.ShapeDtypeStruct((count, T...  23.1 us
  transfers between devices with their start and end apart: 7, of which 4 were waited for; matrix products, arithmetic and copies ran while one was open for 43% of the time, Pallas kernels for 3%

profile of v1, /device:TPU:0, one launch (start us, length us, event | category | flops | bytes accessed | tf_op | source)
XLA Modules:
  0.0 759.4 jit_solution(17841694667528367400)
XLA Ops:
  9.7 18.4 %bitcast_subtract_fusion.src = f32[512,2048]{1,0:T(8,128)} fusion(f32[1,512,2048]{2,1,0:T(8,128)} %param.8, bf16[1,2048,4096]{2,1,0:T(8,128)(2,1)} %param.9, s32[]{:T(128)S(6)} %select_n.96), kind=kOutput, calls=%fused_computation.27 | convolution fusion | flops 8590983168 | bytes 29360132 | tf_op jit(solution)/shard_map/dot_general | solution.py:91
  28.2 11.7 %shard_map.55 = f32[4,512,1024]{2,1,0:T(8,128)} custom-call(s32[16]{0:T(128)} %select_reduce_fusion.8.index, s32[16]{0:T(128)} %convert_element_type.15.live, f32[512,2048]{1,0:T(8,128)} %bitcast_subtract_fusion.src), custom_call_target="tpu_custom_call" | custom-call | bytes 12582912 | tf_op jit(solution)/shard_map/pallas_call | solution.py:36
  62.5 76.1 %all-to-all-done = f32[4,512,1024]{2,1,0:T(8,128)} async-done(((f32[4,512,1024]{2,1,0:T(8,128)}), f32[4,512,1024]{2,1,0:T(8,128)}, u32[]{:S(2)}, u32[]{:S(2)}) %all-to-all-start) | async-done | bytes 8388640 | tf_op jit(solution)/shard_map/all_to_all | solution.py:117
  157.0 15.0 %shard_map.58 = f32[16,256,1024]{2,1,0:T(8,128)} custom-call(s32[16]{0:T(128)} %select_reduce_fusion.8.index, s32[16]{0:T(128)} %convert_element_type.15.live, f32[8,256,1024]{2,1,0:T(8,128)} %bitcast.25.src), custom_call_target="tpu_custom_call" | custom-call | bytes 33554432 | tf_op jit(solution)/shard_map/pallas_call | solution.py:52
  172.1 17.6 %copy.70 = f32[4096,1024]{0,1:T(8,128)} copy(f32[4096,1024]{1,0:T(8,128)} %bitcast.155) | data formatting | bytes 33554432 | tf_op jit(solution)/shard_map/reshape | solution.py:62
  189.8 105.6 %all-reduce.5.cloned.1.call-done = f32[1024,1024]{0,1:T(8,128)} async-done(((f32[1024,1024]{0,1:T(8,128)}), f32[1024,1024]{0,1:T(8,128)}) %all-reduce.5.cloned.1.call-update) | async-done | bytes 4194320 | tf_op jit(solution)/shard_map/psum | solution.py:115
  297.5 11.7 %cholesky.214 = f32[128,128]{1,0:T(8,128)S(1)} custom-call(f32[128,128]{1,0:T(8,128)S(1)} %cholesky.346), custom_call_target="Cholesky" | custom-call | tf_op jit(solution)/shard_map/jit(cholesky)/cholesky | solution.py:70
  309.4 9.8 %custom-call.17 = f32[1,128,128]{1,2,0:T(8,128)S(1)} custom-call(f32[1,128,128]{2,1,0:T(8,128)S(1)} %get-tuple-element.128), custom_call_target="InvertDiagBlocksLowerTriangular" | custom-call | tf_op jit(solution)/shard_map/jit(cholesky)/cholesky | solution.py:70
  319.8 11.7 %cholesky.231 = f32[128,128]{1,0:T(8,128)S(1)} custom-call(f32[128,128]{1,0:T(8,128)S(1)} %convolution_subtract_fusion.9), custom_call_target="Cholesky" | custom-call | tf_op jit(solution)/shard_map/jit(cholesky)/cholesky | solution.py:70
  338.4 20.1 %custom-call.18 = f32[2,128,128]{1,2,0:T(8,128)S(1)} custom-call(f32[2,128,128]{2,1,0:T(8,128)S(1)} %get-tuple-element.33), custom_call_target="InvertDiagBlocksLowerTriangular" | custom-call | tf_op jit(solution)/shard_map/triangular_solve/custom-call.0 | solution.py:71
  369.8 13.2 %cholesky.248 = f32[128,128]{1,0:T(8,128)} custom-call(f32[128,128]{1,0:T(8,128)} %cholesky.349), custom_call_target="Cholesky" | custom-call | tf_op jit(solution)/shard_map/jit(cholesky)/cholesky | solution.py:70
  386.1 11.3 %custom-call.19 = f32[1,128,128]{1,2,0:T(8,128)} custom-call(f32[1,128,128]{2,1,0:T(8,128)} %get-tuple-element.126), custom_call_target="InvertDiagBlocksLowerTriangular" | custom-call | tf_op jit(solution)/shard_map/jit(cholesky)/cholesky | solution.py:70
  402.4 13.3 %cholesky.265 = f32[128,128]{1,0:T(8,128)} custom-call(f32[128,128]{1,0:T(8,128)} %convolution_subtract_fusion.8), custom_call_target="Cholesky" | custom-call | tf_op jit(solution)/shard_map/jit(cholesky)/cholesky | solution.py:70
  430.1 19.7 %custom-call.20 = f32[2,128,128]{1,2,0:T(8,128)S(1)} custom-call(f32[2,128,128]{2,1,0:T(8,128)S(1)} %get-tuple-element.34), custom_call_target="InvertDiagBlocksLowerTriangular" | custom-call | tf_op jit(solution)/shard_map/triangular_solve/custom-call.0 | solution.py:71
  455.4 11.7 %cholesky.282 = f32[128,128]{1,0:T(8,128)S(1)} custom-call(f32[128,128]{1,0:T(8,128)S(1)} %cholesky.352), custom_call_target="Cholesky" | custom-call | tf_op jit(solution)/shard_map/jit(cholesky)/cholesky | solution.py:70
  467.3 9.8 %custom-call.21 = f32[1,128,128]{1,2,0:T(8,128)S(1)} custom-call(f32[1,128,128]{2,1,0:T(8,128)S(1)} %get-tuple-element.124), custom_call_target="InvertDiagBlocksLowerTriangular" | custom-call | tf_op jit(solution)/shard_map/jit(cholesky)/cholesky | solution.py:70
  477.7 11.7 %cholesky.299 = f32[128,128]{1,0:T(8,128)S(1)} custom-call(f32[128,128]{1,0:T(8,128)S(1)} %convolution_subtract_fusion.7), custom_call_target="Cholesky" | custom-call | tf_op jit(solution)/shard_map/jit(cholesky)/cholesky | solution.py:70
  497.7 19.7 %custom-call.22 = f32[2,128,128]{1,2,0:T(8,128)S(1)} custom-call(f32[2,128,128]{2,1,0:T(8,128)S(1)} %get-tuple-element.35), custom_call_target="InvertDiagBlocksLowerTriangular" | custom-call | tf_op jit(solution)/shard_map/triangular_solve/custom-call.0 | solution.py:71
  521.1 11.7 %cholesky.316 = f32[128,128]{1,0:T(8,128)S(1)} custom-call(f32[128,128]{1,0:T(8,128)S(1)} %cholesky.355), custom_call_target="Cholesky" | custom-call | tf_op jit(solution)/shard_map/jit(cholesky)/cholesky | solution.py:70
  533.0 9.8 %custom-call.23 = f32[1,128,128]{1,2,0:T(8,128)S(1)} custom-call(f32[1,128,128]{2,1,0:T(8,128)S(1)} %get-tuple-element.122), custom_call_target="InvertDiagBlocksLowerTriangular" | custom-call | tf_op jit(solution)/shard_map/jit(cholesky)/cholesky | solution.py:70
  543.4 11.7 %cholesky.333 = f32[128,128]{1,0:T(8,128)S(1)} custom-call(f32[128,128]{1,0:T(8,128)S(1)} %convolution_subtract_fusion.6), custom_call_target="Cholesky" | custom-call | tf_op jit(solution)/shard_map/jit(cholesky)/cholesky | solution.py:70
  577.3 19.7 %custom-call.24 = f32[2,128,128]{1,2,0:T(8,128)S(1)} custom-call(f32[2,128,128]{2,1,0:T(8,128)S(1)} %get-tuple-element.36), custom_call_target="InvertDiagBlocksLowerTriangular" | custom-call | tf_op jit(solution)/shard_map/triangular_solve/custom-call.0 | solution.py:71
  619.5 120.7 %reduce-scatter.2.cloned.1.call-done = f32[512,1024]{0,1:T(8,128)} async-done(((f32[4096,1024]{0,1:T(8,128)}), f32[512,1024]{0,1:T(8,128)}) %reduce-scatter.2.cloned.1.call-update) | async-done | bytes 2097168 | tf_op jit(solution)/shard_map/reduce_scatter | solution.py:126
  740.3 9.6 %fusion.16 = f32[512,1024]{0,1:T(8,128)} fusion(s32[]{:T(128)S(6)} %select_n.98, f32[256,256]{0,1:T(8,128)} %get-tuple-element.108, f32[768,256]{0,1:T(8,128)S(1)} %copy.47, f32[256,256]{0,1:T(8,128)S(1)} %cholesky.243, f32[256,256]{0,1:T(8,128)} %get-tuple-element.106, f32[512,256]{0,1:T(8,128)} %copy.54, f32[512,256]{0,1:T(8,128)S(1)} %broadcast_in_dim.36, ...), kind=kOutput, calls=%fused_computation.36 | convolution fusion | flops 3235381248 | bytes 28573702 | tf_op jit(solution)/shard_map/dot_general | solution.py:17
  (218 shorter events, 166.1 us)
Async XLA Ops:
  39.8 98.8 %all-to-all-start = ((f32[4,512,1024]{2,1,0:T(8,128)}), f32[4,512,1024]{2,1,0:T(8,128)}, u32[]{:S(2)}, u32[]{:S(2)}) async-start(f32[4,512,1024]{2,1,0:T(8,128)} %shard_map.55), calls=%async_computation | async-start | bytes 16777216 | tf_op jit(solution)/shard_map/all_to_all | solution.py:117
  45.5 249.9 %all-reduce.5.cloned.1.call-start = ((), (), s32[]{:S(2)}) async-start(), calls=%async_computation.2 | async-start | bytes 8388608 | tf_op jit(solution)/shard_map/psum | solution.py:115
  45.6 3.2 copy-start.18
  45.6 3.2 copy-start.19
  55.2 5.5 copy-start.6
  153.3 401.9 %all-reduce.7.cloned.1.call-start = ((), (), s32[]{:S(2)}) async-start(), calls=%async_computation.3 | async-start | bytes 8388608 | tf_op jit(solution)/shard_map/psum | solution.py:124
  156.8 583.4 %reduce-scatter.2.cloned.1.call-start = ((), (), s32[]{:S(2)}) async-start(), calls=%async_computation.4 | async-start | bytes 18874368 | tf_op jit(solution)/shard_map/reduce_scatter | solution.py:126
  364.8 59.3 %copy-start.1 = (f32[768,768]{0,1:T(8,128)}, f32[768,768]{0,1:T(8,128)S(1)}, u32[]{:S(2)}) copy-start(f32[768,768]{0,1:T(8,128)S(1)} %slice_subtract_fusion.1) | copy-start | bytes 7077892
  368.5 0.7 copy-start.15
  451.6 3.6 copy-start.11
  518.1 14.9 %copy-start.7 = (f32[128,256]{1,0:T(8,128)}, f32[128,256]{1,0:T(8,128)S(1)}, u32[]{:S(2)}) copy-start(f32[128,256]{1,0:T(8,128)S(1)} %fusion.52) | copy-start | bytes 393220
  558.3 39.7 %collective-permute-start = (f32[1024,512]{1,0:T(8,128)}, f32[1024,512]{1,0:T(8,128)}, u32[]{:S(2)}, u32[]{:S(2)}) collective-permute-start(f32[1024,512]{1,0:T(8,128)} %constant_dynamic-slice_fusion.4), channel_id=1, source_target_pairs={{0,3},{4,7},{9,8},{13,12},{18,17},{22,21},{27,26},{31,30}} | collective-permute-start | bytes 6291464 | tf_op jit(solution)/shard_map/ppermute | solution.py:135
  560.9 45.0 %collective-permute-start.1 = (f32[1024,512]{1,0:T(8,128)}, f32[1024,512]{1,0:T(8,128)}, u32[]{:S(2)}, u32[]{:S(2)}) collective-permute-start(f32[1024,512]{1,0:T(8,128)} %constant_dynamic-slice_fusion.4), channel_id=1, source_target_pairs={{0,2},{4,6},{9,11},{13,15},{18,16},{22,20},{27,25},{31,29}} | collective-permute-start | bytes 6291464 | tf_op jit(solution)/shard_map/ppermute | solution.py:135
  565.0 40.9 %collective-permute-start.2 = (f32[1024,512]{1,0:T(8,128)}, f32[1024,512]{1,0:T(8,128)}, u32[]{:S(2)}, u32[]{:S(2)}) collective-permute-start(f32[1024,512]{1,0:T(8,128)} %constant_dynamic-slice_fusion.4), channel_id=1, source_target_pairs={{0,1},{4,5},{9,10},{13,14},{18,19},{22,23},{27,24},{31,28}} | collective-permute-start | bytes 6291464 | tf_op jit(solution)/shard_map/ppermute | solution.py:135
  598.0 10.7 %copy-start.10 = (f32[128,256]{1,0:T(8,128)S(1)}, f32[128,256]{1,0:T(8,128)}, u32[]{:S(2)}) copy-start(f32[128,256]{1,0:T(8,128)} %copy-done.9) | copy-start | bytes 393220
  605.9 2.8 copy-start
  609.6 2.3 copy-start.4
  609.6 2.3 copy-start.12
  612.8 1.6 copy-start.3
  612.8 1.6 copy-start.8
  612.8 1.6 copy-start.14
  615.3 1.2 copy-start.5
  617.4 122.9 %copy-start.2 = (f32[512,1024]{0,1:T(8,128)S(1)}, f32[512,1024]{0,1:T(8,128)}, u32[]{:S(2)}) copy-start(f32[512,1024]{0,1:T(8,128)} %copy.41) | copy-start | bytes 6291460
  617.4 122.9 %copy-start.16 = (f32[256,256]{0,1:T(8,128)S(1)}, f32[256,256]{0,1:T(8,128)}, u32[]{:S(2)}) copy-start(f32[256,256]{0,1:T(8,128)} %copy.61) | copy-start | bytes 786436
  (3 other events, 1.9 us)
Sparse Core Ops, SparseCore 0:
  153.4 141.9 all-reduce.4
  299.1 155.5 all-reduce.6
  458.4 281.6 reduce-scatter.1

commit v2 on v1

--- a/solution.py
+++ b/solution.py
@@ -2,6 +2,7 @@
 
 import jax
 import jax.numpy as jnp
+import numpy as np
 from jax import lax
 from jax.experimental import pallas as pl
 from jax.experimental.pallas import tpu as pltpu
@@ -10,6 +11,7 @@
 TILE = 256
 STEPS = 4
 SPAN = STEPS * TILE
+BLOCK = 128
 HIGH = lax.Precision.HIGH
 
 
@@ -62,15 +64,37 @@
     )(index, live, tiles).reshape(count * TILE, width)
 
 
+def place_parts(tiles, index, part, live, rows):
+    count = index.shape[0]
+    width = tiles.shape[2]
+
+    def body(index, part, live, src, dst):
+        copy_tile(index, live, src, dst)
+
+    return pl.pallas_call(
+        body,
+        out_shape=jax.ShapeDtypeStruct((count * rows, width), jnp.float32),
+        grid_spec=pltpu.PrefetchScalarGridSpec(
+            num_scalar_prefetch=3,
+            grid=(count,),
+            in_specs=[
+                pl.BlockSpec((1, rows, width), lambda f, index, part, live: (index[f], part[f], 0))
+            ],
+            out_specs=pl.BlockSpec((rows, width), lambda f, index, part, live: (f, 0)),
+        ),
+        cost_estimate=pl.CostEstimate(flops=0, bytes_accessed=8 * count * rows * width, transcendentals=0),
+    )(index, part, live, tiles)
+
+
 def factorize(top):
-    eye = jnp.eye(TILE, dtype=jnp.float32)
+    eye = jnp.eye(BLOCK, dtype=jnp.float32)
     work = top
     columns, inverses = [], []
-    for _ in range(STEPS):
-        diag = jnp.linalg.cholesky(work[:TILE, :TILE])
+    for _ in range(SPAN // BLOCK):
+        diag = lax.linalg.cholesky(work[:BLOCK, :BLOCK], symmetrize_input=False)
         inv = lax.linalg.triangular_solve(diag, eye, left_side=True, lower=True)
-        lower = mm(work[TILE:, :TILE], inv, ((1,), (1,)))
-        work = work[TILE:, TILE:] - mm(lower, lower, ((1,), (1,)))
+        lower = mm(work[BLOCK:, :BLOCK], inv, ((1,), (1,)))
+        work = work[BLOCK:, BLOCK:] - mm(lower, lower, ((1,), (1,)))
         columns.append((diag, lower))
         inverses.append(inv)
     return columns, inverses
@@ -98,22 +122,8 @@
     index = jnp.sum(jnp.where(hit, positions[None, :], 0), axis=1).astype(jnp.int32)
 
     placed = place_columns(update, index, live, panels)
-    pivot_panels = SPAN // width
-    left = jnp.concatenate([placed[i] for i in range(pivot_panels)], axis=1)
-    own = index[:STEPS] - panel_id * own_tiles
-    held = (live[:STEPS] > 0) & (own >= 0) & (own < own_tiles)
-    top_part = place_rows(
-        left.reshape(own_tiles, TILE, SPAN),
-        jnp.where(held, own, 0).astype(jnp.int32),
-        held.astype(jnp.int32),
-    )
-    own_top = jnp.where(is_top & is_left, parent_front, 0.0)
     row_clip = jnp.where(is_top, row_start, 0)
     col_clip = jnp.where(is_left, col_start, 0)
-    old = lax.dynamic_slice(top_part, (row_clip, col_clip), (height, width))
-    top_part = lax.dynamic_update_slice(top_part, old + own_top, (row_clip, col_clip))
-    top = lax.psum(top_part, ("leaf", "panel"))
-
     moved = lax.all_to_all(placed, "panel", split_axis=0, concat_axis=0, tiled=True)
     moved = moved.reshape(child_tiles, TILE, width)
     pivot_part = place_rows(moved, index[:STEPS], live[:STEPS])
@@ -122,8 +132,31 @@
         pivot_part, old + jnp.where(is_top, parent_front, 0.0), (row_clip, 0)
     )
     pivot_rows = lax.psum(pivot_part, "leaf")
-    expanded = place_rows(moved, index, live)
-    front_block = parent_front + lax.psum_scatter(expanded, "leaf", scatter_dimension=0, tiled=True)
+    tops = SPAN // height
+    tail = height * tops // leaves
+    head = height - tail
+    served = head // tail
+    order_rows = []
+    for l in range(leaves):
+        if l < tops:
+            order_rows += [(tops + l * served + i) * height + head for i in range(served)]
+        else:
+            order_rows += [l * height + i * tail for i in range(served)]
+    order_rows = np.array(order_rows)
+    expanded = place_parts(
+        moved,
+        index[order_rows // TILE],
+        jnp.asarray(order_rows % TILE // tail, jnp.int32),
+        live[order_rows // TILE],
+        tail,
+    )
+    summed = lax.psum_scatter(expanded, "leaf", scatter_dimension=0, tiled=True)
+    end = jnp.zeros((tail, width), jnp.float32)
+    for i in range(served):
+        pairs = [(l, tops + l * served + i) for l in range(tops)]
+        got = lax.ppermute(summed[i * tail : (i + 1) * tail], "leaf", pairs)
+        end = jnp.where(lax.rem(leaf_id - tops + served * leaves, served) == i, got, end)
+    front_block = parent_front + jnp.concatenate([summed, end], axis=0)
 
     mine = lax.dynamic_slice(pivot_rows, (0, lax.rem(row_start, width)), (SPAN, height))
     source = [l * height // width for l in range(leaves)]
@@ -136,20 +169,43 @@
         holder = row_start // width
         own_cols = jnp.where(lax.rem(holder + shift, panels) == panel_id, got, own_cols)
 
-    columns, inverses = factorize(top)
+    pieces = []
+    for root in range(SPAN // width):
+        local = range(width // TILE)
+        value = jnp.concatenate(
+            [
+                pivot_rows[(root * width + k * TILE) :, k * TILE : (k + 1) * TILE]
+                for k in local
+            ],
+            axis=0,
+        )
+        holders, step = [root], panels // 2
+        while step:
+            got = lax.ppermute(value, "panel", [(h, h ^ step) for h in holders])
+            reached = [h ^ step for h in holders]
+            takes = functools.reduce(jnp.logical_or, [panel_id == h for h in reached])
+            value = jnp.where(takes, got, value)
+            holders, step = holders + reached, step // 2
+        at = 0
+        for k in local:
+            above = root * width + k * TILE
+            piece = value[at : at + SPAN - above]
+            at += SPAN - above
+            pieces.append(jnp.concatenate([jnp.zeros((above, TILE), jnp.float32), piece], axis=0))
+    columns, inverses = factorize(jnp.concatenate(pieces, axis=1))
     rhs = jnp.concatenate([pivot_rows, own_cols], axis=1)
     solved = []
-    for k in range(STEPS):
-        solved.append(mm(inverses[k], rhs[:TILE], ((1,), (0,))))
-        if k < STEPS - 1:
-            rhs = rhs[TILE:] - mm(columns[k][1], solved[k], ((1,), (0,)))
+    for k, inverse in enumerate(inverses):
+        solved.append(mm(inverse, rhs[:BLOCK], ((1,), (0,))))
+        if k + 1 < len(inverses):
+            rhs = rhs[BLOCK:] - mm(columns[k][1], solved[k], ((1,), (0,)))
     solved = jnp.concatenate(solved, axis=0)
     below_cols, below_rows = solved[:, :width], solved[:, width:]
     rest = front_block - mm(below_rows, below_cols, ((0,), (0,)))
 
     factor = jnp.concatenate(
         [
-            jnp.concatenate([jnp.zeros((k * TILE, TILE), jnp.float32), diag, lower], axis=0)
+            jnp.concatenate([jnp.zeros((k * BLOCK, BLOCK), jnp.float32), diag, lower], axis=0)
             for k, (diag, lower) in enumerate(columns)
         ],
         axis=1,

time: 769 us -> 756 us (0.983)
  local copies, waits for them, and re-layouts: 78 us -> 47.6 us
  matrix products: 56.7 us -> 85 us
  other arithmetic: 241 us -> 216 us
  starting transfers between devices: 15.5 us -> 38.4 us
    psum x1, waiting for transfers between devices: 0.02 us -> 140 us  [shards(): pivot_rows = lax.psum(pivot_part, 'leaf')]
    reduce_scatter x1, waiting for transfers between devices: 121 us -> 0.01 us  [shards(): summed = lax.psum_scatter(expanded, 'leaf', scatter_dimension=0, tiled=True)]
    psum x1 -> x0, waiting for transfers between devices: 106 us -> none  [shards(): top = lax.psum(top_part, ('leaf', 'panel'))]
    another operation x27 -> x24, other arithmetic: 145 us -> 101 us  [factorize(): diag = lax.linalg.cholesky(work[:BLOCK, :BLOCK], symmetrize_input=False)]
    ppermute x0 -> x5, waiting for transfers between devices: none -> 43 us  [the longest x2 28 us: shards(): got = lax.ppermute(value, 'panel', [(h, h ^ step) for h in holders])]
    dot_general x14 -> x30, matrix products: 27.9 us -> 63.4 us  [mm(): lax.dot_general(a, b, (dims, ((), ())), precision=HIGH, preferred_element...]
    another operation x72 -> x1, local copies, waits for them, and re-layouts: 27.2 us -> 0.01 us  [factorize(): diag = lax.linalg.cholesky(work[:BLOCK, :BLOCK], symmetrize_input=False)]
    ppermute x3, waiting for transfers between devices: 7.9 us -> 33.9 us  [shards(): got = lax.ppermute(mine, ('leaf', 'panel'), pairs)]
  transfers between devices with their start and end apart: 7 -> 11, of which waited for: 4 -> 8; matrix products, arithmetic and copies ran while one was open for 43% -> 39% of each run, Pallas kernels for 3% -> 2%
where the time goes in v2:
time: 756 us; the launch traced here: 745 us
  waiting for transfers between devices  310 us (41%)
  other arithmetic  216 us (29%)
  matrix products  85 us (11%)
  local copies, waits for them, and re-layouts  47.6 us (6%)
  starting transfers between devices  38.4 us (5%)
  Pallas kernels  32.7 us (4%)
  between operations  15.6 us (2%)
    psum x1, waiting for transfers between devices, shards(): pivot_rows = lax.psum(pivot_part, 'leaf')  140 us
    another operation x24, other arithmetic, factorize(): diag = lax.linalg.cholesky(work[:BLOCK, :BLOCK], symmetrize_input=False)  101 us
    all_to_all x1, waiting for transfers between devices, shards(): lax.all_to_all(placed, 'panel', split_axis=0, concat_axis=0, tiled=True)  93.1 us
    another operation x16, other arithmetic, factorize(): inv = lax.linalg.triangular_solve(diag, eye, left_side=True, lower=True)  91 us
    dot_general x30, matrix products, mm(): lax.dot_general(a, b, (dims, ((), ())), precision=HIGH, preferred_element...  63.4 us
    ppermute x3, waiting for transfers between devices, shards(): got = lax.ppermute(mine, ('leaf', 'panel'), pairs)  33.9 us
    ppermute x2, waiting for transfers between devices, shards(): got = lax.ppermute(value, 'panel', [(h, h ^ step) for h in holders])  28 us
    unnamed x131, local copies, waits for them, and re-layouts  23.2 us
  transfers between devices with their start and end apart: 11, of which 8 were waited for; matrix products, arithmetic and copies ran while one was open for 39% of the time, Pallas kernels for 2%

profile of v2, /device:TPU:0, one launch (start us, length us, event | category | flops | bytes accessed | tf_op | source)
XLA Modules:
  0.0 745.4 jit_solution(10549291368160694276)
XLA Ops:
  9.8 18.4 %bitcast_subtract_fusion.src = f32[512,2048]{1,0:T(8,128)} fusion(f32[1,512,2048]{2,1,0:T(8,128)} %param.13, bf16[1,2048,4096]{2,1,0:T(8,128)(2,1)} %param.14, s32[]{:T(128)S(6)} %select_n.144), kind=kOutput, calls=%fused_computation.10 | convolution fusion | flops 8590983168 | bytes 29360132 | tf_op jit(solution)/shard_map/dot_general | solution.py:115
  28.2 10.0 %shard_map.100 = f32[4,512,1024]{2,1,0:T(8,128)} custom-call(s32[16]{0:T(128)} %select_reduce_fusion.8.index, s32[16]{0:T(128)} %convert_element_type.20.live, f32[512,2048]{1,0:T(8,128)} %bitcast_subtract_fusion.src), custom_call_target="tpu_custom_call" | custom-call | bytes 12582912 | tf_op jit(solution)/shard_map/pallas_call | solution.py:38
  43.9 93.1 %all-to-all-done = f32[4,512,1024]{2,1,0:T(8,128)} async-done(((f32[4,512,1024]{2,1,0:T(8,128)}), f32[4,512,1024]{2,1,0:T(8,128)}, u32[]{:S(2)}, u32[]{:S(2)}) %all-to-all-start) | async-done | bytes 8388640 | tf_op jit(solution)/shard_map/all_to_all | solution.py:127
  148.1 18.2 %shard_map.102 = f32[3072,1024]{1,0:T(8,128)} custom-call(s32[24]{0:T(128)} %gather_fusion, s32[24]{0:T(128)} %constant.94.clone.part, s32[24]{0:T(128)} %gather_fusion.1, f32[8,256,1024]{2,1,0:T(8,128)} %bitcast.5.src), custom_call_target="tpu_custom_call" | custom-call | bytes 25165824 | tf_op jit(solution)/shard_map/pallas_call | solution.py:74
  166.3 140.4 %all-reduce.6.cloned.1.call-done = f32[1024,1024]{1,0:T(8,128)} async-done(((f32[1024,1024]{1,0:T(8,128)}), f32[1024,1024]{1,0:T(8,128)}) %all-reduce.6.cloned.1.call-update) | async-done | bytes 4194320 | tf_op jit(solution)/shard_map/psum | solution.py:134
  317.8 28.0 %collective-permute-done = f32[2560,256]{1,0:T(8,128)} collective-permute-done((f32[2560,256]{1,0:T(8,128)}, f32[2560,256]{1,0:T(8,128)}, u32[]{:S(2)}, u32[]{:S(2)}) %collective-permute-start) | collective-permute-done | bytes 2621472 | tf_op jit(solution)/shard_map/ppermute | solution.py:184
  364.0 11.4 %collective-permute-done.2 = f32[1024,512]{1,0:T(8,128)} collective-permute-done((f32[1024,512]{1,0:T(8,128)S(1)}, f32[1024,512]{1,0:T(8,128)}, u32[]{:S(2)}, u32[]{:S(2)}) %collective-permute-start.2) | collective-permute-done | bytes 2097184 | tf_op jit(solution)/shard_map/ppermute | solution.py:168
  375.4 22.5 %collective-permute-done.3 = f32[1024,512]{1,0:T(8,128)} collective-permute-done((f32[1024,512]{1,0:T(8,128)S(1)}, f32[1024,512]{1,0:T(8,128)}, u32[]{:S(2)}, u32[]{:S(2)}) %collective-permute-start.3) | collective-permute-done | bytes 2097184 | tf_op jit(solution)/shard_map/ppermute | solution.py:168
  405.2 11.7 %custom-call.20 = f32[128,128]{1,0:T(8,128)S(1)} custom-call(f32[128,128]{1,0:T(8,128)S(1)} %slice.214), custom_call_target="Cholesky" | custom-call | tf_op jit(solution)/shard_map/cholesky/custom-call.1 | solution.py:94
  418.8 9.8 %custom-call.21 = f32[1,128,128]{1,2,0:T(8,128)S(1)} custom-call(f32[1,128,128]{2,1,0:T(8,128)S(1)} %get-tuple-element.21), custom_call_target="InvertDiagBlocksLowerTriangular" | custom-call | tf_op jit(solution)/shard_map/triangular_solve/custom-call.0 | solution.py:95
  435.8 11.7 %custom-call.22 = f32[128,128]{1,0:T(8,128)S(1)} custom-call(f32[128,128]{1,0:T(8,128)S(1)} %slice.220), custom_call_target="Cholesky" | custom-call | tf_op jit(solution)/shard_map/cholesky/custom-call.1 | solution.py:94
  449.4 9.8 %custom-call.23 = f32[1,128,128]{1,2,0:T(8,128)S(1)} custom-call(f32[1,128,128]{2,1,0:T(8,128)S(1)} %get-tuple-element.19), custom_call_target="InvertDiagBlocksLowerTriangular" | custom-call | tf_op jit(solution)/shard_map/triangular_solve/custom-call.0 | solution.py:95
  465.6 11.7 %custom-call.24 = f32[128,128]{1,0:T(8,128)S(1)} custom-call(f32[128,128]{1,0:T(8,128)S(1)} %slice.223), custom_call_target="Cholesky" | custom-call | tf_op jit(solution)/shard_map/cholesky/custom-call.1 | solution.py:94
  479.2 10.0 %custom-call.25 = f32[1,128,128]{1,2,0:T(8,128)S(1)} custom-call(f32[1,128,128]{2,1,0:T(8,128)S(1)} %get-tuple-element.17), custom_call_target="InvertDiagBlocksLowerTriangular" | custom-call | tf_op jit(solution)/shard_map/triangular_solve/custom-call.0 | solution.py:95
  494.4 11.7 %custom-call.26 = f32[128,128]{1,0:T(8,128)S(1)} custom-call(f32[128,128]{1,0:T(8,128)S(1)} %slice.226), custom_call_target="Cholesky" | custom-call | tf_op jit(solution)/shard_map/cholesky/custom-call.1 | solution.py:94
  508.1 9.8 %custom-call.27 = f32[1,128,128]{1,2,0:T(8,128)S(1)} custom-call(f32[1,128,128]{2,1,0:T(8,128)S(1)} %get-tuple-element.15), custom_call_target="InvertDiagBlocksLowerTriangular" | custom-call | tf_op jit(solution)/shard_map/triangular_solve/custom-call.0 | solution.py:95
  522.4 12.1 %custom-call.28 = f32[128,128]{1,0:T(8,128)S(1)} custom-call(f32[128,128]{1,0:T(8,128)S(1)} %slice.229), custom_call_target="Cholesky" | custom-call | tf_op jit(solution)/shard_map/cholesky/custom-call.1 | solution.py:94
  536.6 9.8 %custom-call.29 = f32[1,128,128]{1,2,0:T(8,128)S(1)} custom-call(f32[1,128,128]{2,1,0:T(8,128)S(1)} %get-tuple-element.13), custom_call_target="InvertDiagBlocksLowerTriangular" | custom-call | tf_op jit(solution)/shard_map/triangular_solve/custom-call.0 | solution.py:95
  550.3 11.7 %custom-call.30 = f32[128,128]{1,0:T(8,128)S(1)} custom-call(f32[128,128]{1,0:T(8,128)S(1)} %slice.232), custom_call_target="Cholesky" | custom-call | tf_op jit(solution)/shard_map/cholesky/custom-call.1 | solution.py:94
  563.9 9.8 %custom-call.31 = f32[1,128,128]{1,2,0:T(8,128)S(1)} custom-call(f32[1,128,128]{2,1,0:T(8,128)S(1)} %get-tuple-element.11), custom_call_target="InvertDiagBlocksLowerTriangular" | custom-call | tf_op jit(solution)/shard_map/triangular_solve/custom-call.0 | solution.py:95
  577.9 12.7 %custom-call.32 = f32[128,128]{1,0:T(8,128)S(1)} custom-call(f32[128,128]{1,0:T(8,128)} %slice.235), custom_call_target="Cholesky" | custom-call | tf_op jit(solution)/shard_map/cholesky/custom-call.1 | solution.py:94
  592.4 9.8 %custom-call.33 = f32[1,128,128]{1,2,0:T(8,128)S(1)} custom-call(f32[1,128,128]{2,1,0:T(8,128)S(1)} %get-tuple-element.9), custom_call_target="InvertDiagBlocksLowerTriangular" | custom-call | tf_op jit(solution)/shard_map/triangular_solve/custom-call.0 | solution.py:95
  604.7 12.3 %custom-call.34 = f32[128,128]{1,0:T(8,128)} custom-call(f32[128,128]{1,0:T(8,128)S(1)} %convolution_subtract_fusion.6), custom_call_target="Cholesky" | custom-call | tf_op jit(solution)/shard_map/cholesky/custom-call.1 | solution.py:94
  663.2 11.3 %custom-call.35 = f32[1,128,128]{1,2,0:T(8,128)} custom-call(f32[1,128,128]{2,1,0:T(8,128)} %get-tuple-element.6), custom_call_target="InvertDiagBlocksLowerTriangular" | custom-call | tf_op jit(solution)/shard_map/triangular_solve/custom-call.0 | solution.py:95
  (269 shorter events, 212.1 us)
Async XLA Ops:
  38.2 98.8 %all-to-all-start = ((f32[4,512,1024]{2,1,0:T(8,128)}), f32[4,512,1024]{2,1,0:T(8,128)}, u32[]{:S(2)}, u32[]{:S(2)}) async-start(f32[4,512,1024]{2,1,0:T(8,128)} %shard_map.100), calls=%async_computation | async-start | bytes 16777216 | tf_op jit(solution)/shard_map/all_to_all | solution.py:127
  43.8 262.9 %all-reduce.6.cloned.1.call-start = ((), (), s32[]{:S(2)}) async-start(), calls=%async_computation.2 | async-start | bytes 8388608 | tf_op jit(solution)/shard_map/psum | solution.py:134
  145.0 545.4 %reduce-scatter.2.cloned.1.call-start = ((), (), s32[]{:S(2)}) async-start(), calls=%async_computation.3 | async-start | bytes 14155776 | tf_op jit(solution)/shard_map/reduce_scatter | solution.py:153
  312.9 32.8 %collective-permute-start = (f32[2560,256]{1,0:T(8,128)}, f32[2560,256]{1,0:T(8,128)}, u32[]{:S(2)}, u32[]{:S(2)}) collective-permute-start(f32[2560,256]{1,0:T(8,128)} %pad_maximum_fusion.2), channel_id=1, source_target_pairs={{0,2},{4,6},{8,10},{12,14},{16,18},{20,22},{24,26},{28,30}} | collective-permute-start | bytes 7864328 | tf_op jit(solution)/shard_map/ppermute | solution.py:184
  317.8 32.6 %copy-start.2 = (f32[1024,1024]{1,0:T(8,128)S(1)}, f32[1024,1024]{1,0:T(8,128)}, u32[]{:S(2)}) copy-start(f32[1024,1024]{1,0:T(8,128)} %all-reduce.6.cloned.1.call-done) | copy-start | bytes 12582916
  347.6 53.0 %collective-permute-start.1 = (f32[2560,256]{1,0:T(8,128)}, f32[2560,256]{1,0:T(8,128)}, u32[]{:S(2)}, u32[]{:S(2)}) collective-permute-start(f32[2560,256]{1,0:T(8,128)} %broadcast_select_fusion), channel_id=1, source_target_pairs={{0,1},{2,3},{4,5},{6,7},{8,9},{10,11},{12,13},{14,15},{16,17},{18,... | collective-permute-start | bytes 7864328 | tf_op jit(solution)/shard_map/ppermute | solution.py:184
  350.6 24.8 %collective-permute-start.2 = (f32[1024,512]{1,0:T(8,128)S(1)}, f32[1024,512]{1,0:T(8,128)}, u32[]{:S(2)}, u32[]{:S(2)}) collective-permute-start(f32[1024,512]{1,0:T(8,128)S(1)} %constant_dynamic-slice_fusion), channel_id=1, source_target_pairs={{0,3},{4,7},{9,8},{13,12},{18,17},{22,21},{27,26},{31,30}} | collective-permute-start | bytes 6291464 | tf_op jit(solution)/shard_map/ppermute | solution.py:168
  353.2 44.7 %collective-permute-start.3 = (f32[1024,512]{1,0:T(8,128)S(1)}, f32[1024,512]{1,0:T(8,128)}, u32[]{:S(2)}, u32[]{:S(2)}) collective-permute-start(f32[1024,512]{1,0:T(8,128)S(1)} %constant_dynamic-slice_fusion), channel_id=1, source_target_pairs={{0,2},{4,6},{9,11},{13,15},{18,16},{22,20},{27,25},{31,29}} | collective-permute-start | bytes 6291464 | tf_op jit(solution)/shard_map/ppermute | solution.py:168
  360.1 37.7 %collective-permute-start.4 = (f32[1024,512]{1,0:T(8,128)S(1)}, f32[1024,512]{1,0:T(8,128)}, u32[]{:S(2)}, u32[]{:S(2)}) collective-permute-start(f32[1024,512]{1,0:T(8,128)S(1)} %constant_dynamic-slice_fusion), channel_id=1, source_target_pairs={{0,1},{4,5},{9,10},{13,14},{18,19},{22,23},{27,24},{31,28}} | collective-permute-start | bytes 6291464 | tf_op jit(solution)/shard_map/ppermute | solution.py:168
  489.5 28.4 %copy-start.50 = (f32[128,128]{1,0:T(8,128)}, f32[128,128]{1,0:T(8,128)S(1)}, u32[]{:S(2)}) copy-start(f32[128,128]{1,0:T(8,128)S(1)} %fusion.63) | copy-start | bytes 196612
  490.8 148.2 %copy-start.11 = (f32[640,128]{1,0:T(8,128)}, f32[640,128]{1,0:T(8,128)S(1)}, u32[]{:S(2)}) copy-start(f32[640,128]{1,0:T(8,128)S(1)} %fusion.49) | copy-start | bytes 983044
  518.2 28.2 %copy-start.42 = (f32[128,128]{1,0:T(8,128)}, f32[128,128]{1,0:T(8,128)S(1)}, u32[]{:S(2)}) copy-start(f32[128,128]{1,0:T(8,128)S(1)} %fusion.61) | copy-start | bytes 196612
  519.5 57.1 %copy-start.16 = (f32[512,128]{1,0:T(8,128)}, f32[512,128]{1,0:T(8,128)S(1)}, u32[]{:S(2)}) copy-start(f32[512,128]{1,0:T(8,128)S(1)} %fusion.51) | copy-start | bytes 786436
  522.4 94.7 %copy-start.39 = (f32[128,128]{1,0:T(8,128)S(1)}, f32[128,128]{1,0:T(8,128)}, u32[]{:S(2)}) copy-start(f32[128,128]{1,0:T(8,128)} %copy-done.38) | copy-start | bytes 196612
  546.7 27.1 %copy-start.44 = (f32[128,128]{1,0:T(8,128)}, f32[128,128]{1,0:T(8,128)S(1)}, u32[]{:S(2)}) copy-start(f32[128,128]{1,0:T(8,128)S(1)} %fusion.59) | copy-start | bytes 196612
  547.9 71.6 %copy-start.20 = (f32[384,128]{1,0:T(8,128)}, f32[384,128]{1,0:T(8,128)S(1)}, u32[]{:S(2)}) copy-start(f32[384,128]{1,0:T(8,128)S(1)} %fusion.69) | copy-start | bytes 589828
  574.0 28.2 %copy-start.46 = (f32[128,128]{1,0:T(8,128)}, f32[128,128]{1,0:T(8,128)S(1)}, u32[]{:S(2)}) copy-start(f32[128,128]{1,0:T(8,128)S(1)} %fusion.57) | copy-start | bytes 196612
  575.2 44.2 %copy-start.25 = (f32[256,128]{1,0:T(8,128)}, f32[256,128]{1,0:T(8,128)S(1)}, u32[]{:S(2)}) copy-start(f32[256,128]{1,0:T(8,128)S(1)} %fusion.71) | copy-start | bytes 393220
  659.2 22.5 %copy-start.26 = (f32[256,128]{1,0:T(8,128)S(1)}, f32[256,128]{1,0:T(8,128)}, u32[]{:S(2)}) copy-start(f32[256,128]{1,0:T(8,128)} %copy-done.25) | copy-start | bytes 393220
  661.0 22.8 %copy-start.27 = (f32[128,1536]{0,1:T(8,128)S(1)}, f32[128,1536]{0,1:T(8,128)}, u32[]{:S(2)}) copy-start(f32[128,1536]{0,1:T(8,128)} %copy.27) | copy-start | bytes 2359300
  693.0 20.9 %collective-permute-start.5 = (f32[128,1024]{1,0:T(8,128)}, f32[128,1024]{1,0:T(8,128)S(1)}, u32[]{:S(2)}, u32[]{:S(2)}) collective-permute-start(f32[128,1024]{1,0:T(8,128)} %get-tuple-element.25), channel_id=1, source_target_pairs={{0,16},{4,28},{1,17},{5,29},{2,18},{6,30},{3,19},{7,31}} | collective-permute-start | bytes 1572872 | tf_op jit(solution)/shard_map/ppermute | solution.py:157
  701.3 20.7 %collective-permute-start.6 = (f32[128,1024]{1,0:T(8,128)}, f32[128,1024]{1,0:T(8,128)}, u32[]{:S(2)}, u32[]{:S(2)}) collective-permute-start(f32[128,1024]{1,0:T(8,128)} %get-tuple-element.24), channel_id=1, source_target_pairs={{0,12},{4,24},{1,13},{5,25},{2,14},{6,26},{3,15},{7,27}} | collective-permute-start | bytes 1572872 | tf_op jit(solution)/shard_map/ppermute | solution.py:157
  703.4 24.2 %collective-permute-start.7 = (f32[128,1024]{1,0:T(8,128)}, f32[128,1024]{1,0:T(8,128)}, u32[]{:S(2)}, u32[]{:S(2)}) collective-permute-start(f32[128,1024]{1,0:T(8,128)} %get-tuple-element.23), channel_id=1, source_target_pairs={{0,8},{4,20},{1,9},{5,21},{2,10},{6,22},{3,11},{7,23}} | collective-permute-start | bytes 1572872 | tf_op jit(solution)/shard_map/ppermute | solution.py:157
  706.4 22.4 %copy-start.10 = (f32[512,1024]{1,0:T(8,128)S(1)}, f32[512,1024]{1,0:T(8,128)}, u32[]{:S(2)}) copy-start(f32[512,1024]{1,0:T(8,128)} %param.15) | copy-start | bytes 6291460
  (49 other events, 328.2 us)
Sparse Core Ops, SparseCore 0:
  145.1 161.5 all-reduce.5
  310.3 206.2 reduce-scatter.1

commit v3 on v2

--- a/solution.py
+++ b/solution.py
@@ -86,11 +86,13 @@
     )(index, part, live, tiles)
 
 
-def factorize(top):
+def factorize(top, arrived):
     eye = jnp.eye(BLOCK, dtype=jnp.float32)
     work = top
     columns, inverses = [], []
-    for _ in range(SPAN // BLOCK):
+    for step in range(SPAN // BLOCK):
+        if step == SPAN // BLOCK - 1:
+            work = jnp.where(arrived == arrived, work, 0.0)
         diag = lax.linalg.cholesky(work[:BLOCK, :BLOCK], symmetrize_input=False)
         inv = lax.linalg.triangular_solve(diag, eye, left_side=True, lower=True)
         lower = mm(work[BLOCK:, :BLOCK], inv, ((1,), (1,)))
@@ -157,17 +159,6 @@
         got = lax.ppermute(summed[i * tail : (i + 1) * tail], "leaf", pairs)
         end = jnp.where(lax.rem(leaf_id - tops + served * leaves, served) == i, got, end)
     front_block = parent_front + jnp.concatenate([summed, end], axis=0)
-
-    mine = lax.dynamic_slice(pivot_rows, (0, lax.rem(row_start, width)), (SPAN, height))
-    source = [l * height // width for l in range(leaves)]
-    own_cols = mine
-    for shift in range(1, panels):
-        pairs = [
-            (l * panels + source[l], l * panels + (source[l] + shift) % panels) for l in range(leaves)
-        ]
-        got = lax.ppermute(mine, ("leaf", "panel"), pairs)
-        holder = row_start // width
-        own_cols = jnp.where(lax.rem(holder + shift, panels) == panel_id, got, own_cols)
 
     pieces = []
     for root in range(SPAN // width):
@@ -192,7 +183,19 @@
             piece = value[at : at + SPAN - above]
             at += SPAN - above
             pieces.append(jnp.concatenate([jnp.zeros((above, TILE), jnp.float32), piece], axis=0))
-    columns, inverses = factorize(jnp.concatenate(pieces, axis=1))
+    columns, inverses = factorize(jnp.concatenate(pieces, axis=1), end[0, 0])
+    mine = lax.dynamic_slice(pivot_rows, (0, lax.rem(row_start, width)), (SPAN, height))
+    source = [l * height // width for l in range(leaves)]
+    mine = jnp.where(columns[0][0][0, 0] > 0, mine, 0.0)
+    own_cols = mine
+    for shift in range(1, panels):
+        pairs = [
+            (l * panels + source[l], l * panels + (source[l] + shift) % panels) for l in range(leaves)
+        ]
+        got = lax.ppermute(mine, ("leaf", "panel"), pairs)
+        holder = row_start // width
+        own_cols = jnp.where(lax.rem(holder + shift, panels) == panel_id, got, own_cols)
+
     rhs = jnp.concatenate([pivot_rows, own_cols], axis=1)
     solved = []
     for k, inverse in enumerate(inverses):

time: 756 us -> 718 us (0.950)
  waiting for transfers between devices: 310 us -> 284 us
  other arithmetic: 216 us -> 203 us
    ppermute x3, waiting for transfers between devices: 33.9 us -> 0.01 us  [shards(): got = lax.ppermute(mine, ('leaf', 'panel'), pairs)]
    ppermute x3, starting transfers between devices: 12.6 us -> 22.7 us  [shards(): got = lax.ppermute(mine, ('leaf', 'panel'), pairs)]
    ppermute x3, waiting for transfers between devices: 15 us -> 24.9 us  [shards(): got = lax.ppermute(summed[i * tail:(i + 1) * tail], 'leaf', pairs)]
    ppermute x3, starting transfers between devices: 12.5 us -> 4.14 us  [shards(): got = lax.ppermute(summed[i * tail:(i + 1) * tail], 'leaf', pairs)]
    unnamed x131 -> x113, local copies, waits for them, and re-layouts: 23.2 us -> 29.5 us
  transfers between devices with their start and end apart: 11 -> 11, of which waited for: 8 -> 7; matrix products, arithmetic and copies ran while one was open for 39% -> 35% of each run, Pallas kernels for 2% -> 3%
where the time goes in v3:
time: 718 us; the launch traced here: 712 us
  waiting for transfers between devices  284 us (40%)
  other arithmetic  203 us (28%)
  matrix products  78.3 us (11%)
  local copies, waits for them, and re-layouts  53 us (7%)
  starting transfers between devices  40.2 us (6%)
  Pallas kernels  36.6 us (5%)
  between operations  17.3 us (2%)
    psum x1, waiting for transfers between devices, shards(): pivot_rows = lax.psum(pivot_part, 'leaf')  135 us
    another operation x24, other arithmetic, factorize(): diag = lax.linalg.cholesky(work[:BLOCK, :BLOCK], symmetrize_input=False)  101 us
    all_to_all x1, waiting for transfers between devices, shards(): lax.all_to_all(placed, 'panel', split_axis=0, concat_axis=0, tiled=True)  93.1 us
    another operation x16, other arithmetic, factorize(): inv = lax.linalg.triangular_solve(diag, eye, left_side=True, lower=True)  87.2 us
    dot_general x30, matrix products, mm(): lax.dot_general(a, b, (dims, ((), ())), precision=HIGH, preferred_element...  57.6 us
    ppermute x2, waiting for transfers between devices, shards(): got = lax.ppermute(value, 'panel', [(h, h ^ step) for h in holders])  30.1 us
    unnamed x113, local copies, waits for them, and re-layouts  29.5 us
    ppermute x3, waiting for transfers between devices, shards(): got = lax.ppermute(summed[i * tail:(i + 1) * tail], 'leaf', pairs)  24.9 us
  transfers between devices with their start and end apart: 11, of which 7 were waited for; matrix products, arithmetic and copies ran while one was open for 35% of the time, Pallas kernels for 3%

profile of v3, /device:TPU:0, one launch (start us, length us, event | category | flops | bytes accessed | tf_op | source)
XLA Modules:
  0.0 712.1 jit_solution(12958239840646903551)
XLA Ops:
  9.8 18.4 %bitcast_subtract_fusion.src = f32[512,2048]{1,0:T(8,128)} fusion(f32[1,512,2048]{2,1,0:T(8,128)} %param.13, bf16[1,2048,4096]{2,1,0:T(8,128)(2,1)} %param.14, s32[]{:T(128)S(6)} %select_n.160), kind=kOutput, calls=%fused_computation.10 | convolution fusion | flops 8590983168 | bytes 29360132 | tf_op jit(solution)/shard_map/dot_general | solution.py:117
  28.2 12.6 %shard_map.100 = f32[4,512,1024]{2,1,0:T(8,128)} custom-call(s32[16]{0:T(128)} %select_reduce_fusion.8.index, s32[16]{0:T(128)} %convert_element_type.20.live, f32[512,2048]{1,0:T(8,128)} %bitcast_subtract_fusion.src), custom_call_target="tpu_custom_call" | custom-call | bytes 12582912 | tf_op jit(solution)/shard_map/pallas_call | solution.py:38
  46.5 93.1 %all-to-all-done = f32[4,512,1024]{2,1,0:T(8,128)} async-done(((f32[4,512,1024]{2,1,0:T(8,128)}), f32[4,512,1024]{2,1,0:T(8,128)}, u32[]{:S(2)}, u32[]{:S(2)}) %all-to-all-start) | async-done | bytes 8388640 | tf_op jit(solution)/shard_map/all_to_all | solution.py:129
  151.9 18.2 %shard_map.102 = f32[3072,1024]{1,0:T(8,128)} custom-call(s32[24]{0:T(128)} %gather_fusion, s32[24]{0:T(128)} %constant.96.clone.part, s32[24]{0:T(128)} %gather_fusion.1, f32[8,256,1024]{2,1,0:T(8,128)} %bitcast.5.src), custom_call_target="tpu_custom_call" | custom-call | bytes 25165824 | tf_op jit(solution)/shard_map/pallas_call | solution.py:74
  170.1 135.4 %all-reduce.6.cloned.1.call-done = f32[1024,1024]{1,0:T(8,128)} async-done(((f32[1024,1024]{1,0:T(8,128)}), f32[1024,1024]{1,0:T(8,128)}) %all-reduce.6.cloned.1.call-update) | async-done | bytes 4194320 | tf_op jit(solution)/shard_map/psum | solution.py:136
  316.4 27.7 %collective-permute-done = f32[2560,256]{1,0:T(8,128)} collective-permute-done((f32[2560,256]{1,0:T(8,128)S(1)}, f32[2560,256]{1,0:T(8,128)}, u32[]{:S(2)}, u32[]{:S(2)}) %collective-permute-start) | collective-permute-done | bytes 2621472 | tf_op jit(solution)/shard_map/ppermute | solution.py:175
  356.6 11.7 %custom-call.20 = f32[128,128]{1,0:T(8,128)S(1)} custom-call(f32[128,128]{1,0:T(8,128)S(1)} %slice.222), custom_call_target="Cholesky" | custom-call | tf_op jit(solution)/shard_map/cholesky/custom-call.1 | solution.py:96
  384.0 13.4 %collective-permute-start.7 = (f32[1024,512]{1,0:T(8,128)}, f32[1024,512]{1,0:T(8,128)}, u32[]{:S(2)}, u32[]{:S(2)}) collective-permute-start(f32[1024,512]{1,0:T(8,128)} %dynamic-slice_select_fusion), channel_id=1, source_target_pairs={{0,1},{4,5},{9,10},{13,14},{18,19},{22,23},{27,24},{31,28}} | collective-permute-start | bytes 6291464 | tf_op jit(solution)/shard_map/ppermute | solution.py:195
  397.3 9.8 %custom-call.21 = f32[1,128,128]{1,2,0:T(8,128)S(1)} custom-call(f32[1,128,128]{2,1,0:T(8,128)S(1)} %get-tuple-element.21), custom_call_target="InvertDiagBlocksLowerTriangular" | custom-call | tf_op jit(solution)/shard_map/triangular_solve/custom-call.0 | solution.py:97
  413.1 11.7 %custom-call.22 = f32[128,128]{1,0:T(8,128)S(1)} custom-call(f32[128,128]{1,0:T(8,128)S(1)} %slice.228), custom_call_target="Cholesky" | custom-call | tf_op jit(solution)/shard_map/cholesky/custom-call.1 | solution.py:96
  426.8 9.8 %custom-call.23 = f32[1,128,128]{1,2,0:T(8,128)S(1)} custom-call(f32[1,128,128]{2,1,0:T(8,128)S(1)} %get-tuple-element.19), custom_call_target="InvertDiagBlocksLowerTriangular" | custom-call | tf_op jit(solution)/shard_map/triangular_solve/custom-call.0 | solution.py:97
  443.0 11.7 %custom-call.24 = f32[128,128]{1,0:T(8,128)S(1)} custom-call(f32[128,128]{1,0:T(8,128)S(1)} %slice.231), custom_call_target="Cholesky" | custom-call | tf_op jit(solution)/shard_map/cholesky/custom-call.1 | solution.py:96
  456.8 10.2 %custom-call.25 = f32[1,128,128]{1,2,0:T(8,128)S(1)} custom-call(f32[1,128,128]{2,1,0:T(8,128)S(1)} %get-tuple-element.17), custom_call_target="InvertDiagBlocksLowerTriangular" | custom-call | tf_op jit(solution)/shard_map/triangular_solve/custom-call.0 | solution.py:97
  471.5 11.7 %custom-call.26 = f32[128,128]{1,0:T(8,128)S(1)} custom-call(f32[128,128]{1,0:T(8,128)S(1)} %slice.234), custom_call_target="Cholesky" | custom-call | tf_op jit(solution)/shard_map/cholesky/custom-call.1 | solution.py:96
  485.1 9.8 %custom-call.27 = f32[1,128,128]{1,2,0:T(8,128)S(1)} custom-call(f32[1,128,128]{2,1,0:T(8,128)S(1)} %get-tuple-element.15), custom_call_target="InvertDiagBlocksLowerTriangular" | custom-call | tf_op jit(solution)/shard_map/triangular_solve/custom-call.0 | solution.py:97
  497.2 11.9 %custom-call.28 = f32[128,128]{1,0:T(8,128)S(1)} custom-call(f32[128,128]{1,0:T(8,128)S(1)} %slice.237), custom_call_target="Cholesky" | custom-call | tf_op jit(solution)/shard_map/cholesky/custom-call.1 | solution.py:96
  510.3 9.8 %custom-call.29 = f32[1,128,128]{1,2,0:T(8,128)S(1)} custom-call(f32[1,128,128]{2,1,0:T(8,128)S(1)} %get-tuple-element.13), custom_call_target="InvertDiagBlocksLowerTriangular" | custom-call | tf_op jit(solution)/shard_map/triangular_solve/custom-call.0 | solution.py:97
  523.2 11.7 %custom-call.30 = f32[128,128]{1,0:T(8,128)S(1)} custom-call(f32[128,128]{1,0:T(8,128)S(1)} %slice.240), custom_call_target="Cholesky" | custom-call | tf_op jit(solution)/shard_map/cholesky/custom-call.1 | solution.py:96
  536.3 9.8 %custom-call.31 = f32[1,128,128]{1,2,0:T(8,128)S(1)} custom-call(f32[1,128,128]{2,1,0:T(8,128)S(1)} %get-tuple-element.11), custom_call_target="InvertDiagBlocksLowerTriangular" | custom-call | tf_op jit(solution)/shard_map/triangular_solve/custom-call.0 | solution.py:97
  547.0 11.9 %custom-call.32 = f32[128,128]{1,0:T(8,128)S(1)} custom-call(f32[128,128]{1,0:T(8,128)S(1)} %slice.243), custom_call_target="Cholesky" | custom-call | tf_op jit(solution)/shard_map/cholesky/custom-call.1 | solution.py:96
  560.2 9.8 %custom-call.33 = f32[1,128,128]{1,2,0:T(8,128)S(1)} custom-call(f32[1,128,128]{2,1,0:T(8,128)S(1)} %get-tuple-element.9), custom_call_target="InvertDiagBlocksLowerTriangular" | custom-call | tf_op jit(solution)/shard_map/triangular_solve/custom-call.0 | solution.py:97
  645.2 11.2 %collective-permute-done.3 = f32[128,1024]{1,0:T(8,128)S(1)} collective-permute-done((f32[128,1024]{1,0:T(8,128)S(1)}, f32[128,1024]{1,0:T(8,128)S(1)}, u32[]{:S(2)}, u32[]{:S(2)}) %collective-permute-start.3) | collective-permute-done | bytes 524320 | tf_op jit(solution)/shard_map/ppermute | solution.py:159
  667.8 12.5 %custom-call.34 = f32[128,128]{1,0:T(8,128)S(1)} custom-call(f32[128,128]{1,0:T(8,128)} %broadcast_select_fusion.2), custom_call_target="Cholesky" | custom-call | tf_op jit(solution)/shard_map/cholesky/custom-call.1 | solution.py:96
  682.2 10.6 %custom-call.35 = f32[1,128,128]{1,2,0:T(8,128)S(1)} custom-call(f32[1,128,128]{2,1,0:T(8,128)} %get-tuple-element.6), custom_call_target="InvertDiagBlocksLowerTriangular" | custom-call | tf_op jit(solution)/shard_map/triangular_solve/custom-call.0 | solution.py:97
  (253 shorter events, 190.2 us)
Async XLA Ops:
  40.8 98.8 %all-to-all-start = ((f32[4,512,1024]{2,1,0:T(8,128)}), f32[4,512,1024]{2,1,0:T(8,128)}, u32[]{:S(2)}, u32[]{:S(2)}) async-start(f32[4,512,1024]{2,1,0:T(8,128)} %shard_map.100), calls=%async_computation | async-start | bytes 16777216 | tf_op jit(solution)/shard_map/all_to_all | solution.py:129
  46.4 259.1 %all-reduce.6.cloned.1.call-start = ((), (), s32[]{:S(2)}) async-start(), calls=%async_computation.2 | async-start | bytes 8388608 | tf_op jit(solution)/shard_map/psum | solution.py:136
  148.7 481.3 %reduce-scatter.2.cloned.1.call-start = ((), (), s32[]{:S(2)}) async-start(), calls=%async_computation.3 | async-start | bytes 14155776 | tf_op jit(solution)/shard_map/reduce_scatter | solution.py:155
  311.5 32.5 %collective-permute-start = (f32[2560,256]{1,0:T(8,128)S(1)}, f32[2560,256]{1,0:T(8,128)}, u32[]{:S(2)}, u32[]{:S(2)}) collective-permute-start(f32[2560,256]{1,0:T(8,128)S(1)} %pad_maximum_fusion.2), channel_id=1, source_target_pairs={{0,2},{4,6},{8,10},{12,14},{16,18},{20,22},{24,26},{28,30}} | collective-permute-start | bytes 7864328 | tf_op jit(solution)/shard_map/ppermute | solution.py:175
  345.9 5.9 collective-permute-start.1
  374.7 197.2 %collective-permute-start.5 = (f32[1024,512]{1,0:T(8,128)}, f32[1024,512]{1,0:T(8,128)}, u32[]{:S(2)}, u32[]{:S(2)}) collective-permute-start(f32[1024,512]{1,0:T(8,128)} %dynamic-slice_select_fusion), channel_id=1, source_target_pairs={{0,3},{4,7},{9,8},{13,12},{18,17},{22,21},{27,26},{31,30}} | collective-permute-start | bytes 6291464 | tf_op jit(solution)/shard_map/ppermute | solution.py:195
  381.3 190.5 %collective-permute-start.6 = (f32[1024,512]{1,0:T(8,128)}, f32[1024,512]{1,0:T(8,128)}, u32[]{:S(2)}, u32[]{:S(2)}) collective-permute-start(f32[1024,512]{1,0:T(8,128)} %dynamic-slice_select_fusion), channel_id=1, source_target_pairs={{0,2},{4,6},{9,11},{13,15},{18,16},{22,20},{27,25},{31,29}} | collective-permute-start | bytes 6291464 | tf_op jit(solution)/shard_map/ppermute | solution.py:195
  384.0 189.9 %collective-permute-start.7 = (f32[1024,512]{1,0:T(8,128)}, f32[1024,512]{1,0:T(8,128)}, u32[]{:S(2)}, u32[]{:S(2)}) collective-permute-start(f32[1024,512]{1,0:T(8,128)} %dynamic-slice_select_fusion), channel_id=1, source_target_pairs={{0,1},{4,5},{9,10},{13,14},{18,19},{22,23},{27,24},{31,28}} | collective-permute-start | bytes 6291464 | tf_op jit(solution)/shard_map/ppermute | solution.py:195
  495.2 24.9 %copy-start.34 = (f32[128,128]{1,0:T(8,128)}, f32[128,128]{1,0:T(8,128)S(1)}, u32[]{:S(2)}) copy-start(f32[128,128]{1,0:T(8,128)S(1)} %fusion.61) | copy-start | bytes 196612
  495.5 74.5 %copy-start.19 = (f32[896,128]{1,0:T(8,128)S(1)}, f32[896,128]{1,0:T(8,128)}, u32[]{:S(2)}) copy-start(f32[896,128]{1,0:T(8,128)} %copy-done.18) | copy-start | bytes 1376260
  497.2 72.9 %copy-start.48 = (f32[128,128]{1,0:T(8,128)S(1)}, f32[128,128]{1,0:T(8,128)}, u32[]{:S(2)}) copy-start(f32[128,128]{1,0:T(8,128)} %copy-done.47) | copy-start | bytes 196612
  497.2 73.0 %copy-start.49 = (f32[128,128]{1,0:T(8,128)S(1)}, f32[128,128]{1,0:T(8,128)}, u32[]{:S(2)}) copy-start(f32[128,128]{1,0:T(8,128)} %get-tuple-element.20) | copy-start | bytes 196612
  520.4 49.8 %copy-start.36 = (f32[128,128]{1,0:T(8,128)}, f32[128,128]{1,0:T(8,128)S(1)}, u32[]{:S(2)}) copy-start(f32[128,128]{1,0:T(8,128)S(1)} %fusion.59) | copy-start | bytes 196612
  520.4 50.3 %copy-start.46 = (f32[128,128]{1,0:T(8,128)S(1)}, f32[128,128]{1,0:T(8,128)}, u32[]{:S(2)}) copy-start(f32[128,128]{1,0:T(8,128)} %get-tuple-element.18) | copy-start | bytes 196612
  521.6 49.5 %copy-start.15 = (f32[384,128]{1,0:T(8,128)}, f32[384,128]{1,0:T(8,128)S(1)}, u32[]{:S(2)}) copy-start(f32[384,128]{1,0:T(8,128)S(1)} %fusion.69) | copy-start | bytes 589828
  521.7 49.3 %copy-start.50 = (f32[128,128]{1,0:T(8,128)S(1)}, f32[128,128]{1,0:T(8,128)}, u32[]{:S(2)}) copy-start(f32[128,128]{1,0:T(8,128)} %get-tuple-element.16) | copy-start | bytes 196612
  521.7 49.3 %copy-start.51 = (f32[1024]{0:T(1024)S(1)}, f32[1024]{0:T(1024)}, u32[]{:S(2)}) copy-start(f32[1024]{0:T(1024)} %pad.16.clone) | copy-start | bytes 12292
  546.4 25.0 %copy-start.38 = (f32[128,128]{1,0:T(8,128)}, f32[128,128]{1,0:T(8,128)S(1)}, u32[]{:S(2)}) copy-start(f32[128,128]{1,0:T(8,128)S(1)} %fusion.57) | copy-start | bytes 196612
  546.9 24.9 %copy-start.31 = (f32[256,256]{1,0:T(8,128)}, f32[256,256]{1,0:T(8,128)S(1)}, u32[]{:S(2)}) copy-start(f32[256,256]{1,0:T(8,128)S(1)} %convolution_subtract_fusion.5) | copy-start | bytes 786436
  631.5 13.7 %collective-permute-start.2 = (f32[128,1024]{1,0:T(8,128)S(1)}, f32[128,1024]{1,0:T(8,128)S(1)}, u32[]{:S(2)}, u32[]{:S(2)}) collective-permute-start(f32[128,1024]{1,0:T(8,128)S(1)} %get-tuple-element.25), channel_id=1, source_target_pairs={{0,16},{4,28},{1,17},{5,29},{2,18},{6,30},{3,19},{7,31}} | collective-permute-start | bytes 1572872 | tf_op jit(solution)/shard_map/ppermute | solution.py:159
  632.8 23.6 %collective-permute-start.3 = (f32[128,1024]{1,0:T(8,128)S(1)}, f32[128,1024]{1,0:T(8,128)S(1)}, u32[]{:S(2)}, u32[]{:S(2)}) collective-permute-start(f32[128,1024]{1,0:T(8,128)S(1)} %get-tuple-element.24), channel_id=1, source_target_pairs={{0,12},{4,24},{1,13},{5,25},{2,14},{6,26},{3,15},{7,27}} | collective-permute-start | bytes 1572872 | tf_op jit(solution)/shard_map/ppermute | solution.py:159
  634.2 30.0 %collective-permute-start.4 = (f32[128,1024]{1,0:T(8,128)S(1)}, f32[128,1024]{1,0:T(8,128)S(1)}, u32[]{:S(2)}, u32[]{:S(2)}) collective-permute-start(f32[128,1024]{1,0:T(8,128)S(1)} %get-tuple-element.23), channel_id=1, source_target_pairs={{0,8},{4,20},{1,9},{5,21},{2,10},{6,22},{3,11},{7,23}} | collective-permute-start | bytes 1572872 | tf_op jit(solution)/shard_map/ppermute | solution.py:159
  636.7 59.1 %copy-start.10 = (f32[512,1024]{1,0:T(8,128)S(1)}, f32[512,1024]{1,0:T(8,128)}, u32[]{:S(2)}) copy-start(f32[512,1024]{1,0:T(8,128)} %param.15) | copy-start | bytes 6291460
  639.3 54.7 %copy-start.25 = (f32[128,1536]{1,0:T(8,128)S(1)}, f32[128,1536]{1,0:T(8,128)}, u32[]{:S(2)}) copy-start(f32[128,1536]{1,0:T(8,128)} %convolution_subtract_fusion.2) | copy-start | bytes 2359300
  (40 other events, 124.9 us)
Sparse Core Ops, SparseCore 0:
  148.8 156.6 all-reduce.5
  309.1 206.4 reduce-scatter.1
